TPU v7x, 32 devices: a whole 2x2x4 slice. The times are simulated.
32 devices in a mesh: pipe: 2 (over x), row: 8 (over z, core), col: 2 (over y).
Axes of the slice: x: 2, y: 2, z: 4, core: 2. Of those that a mesh axis runs over, the one named last changes fastest.
Arguments:
- inputs: bfloat16 [4, 8, 1024, 512], P(None, 'row', 'col'), may hold values from -6 to 6
- first_gain: float32 [2, 512], P('pipe'), may hold values from 0.5 to 1.5
- first_shift: float32 [2, 512], P('pipe'), may hold values from -1.75 to 1.75
- qkv_weight: bfloat16 [2, 3, 512, 512], P('pipe', None, 'row', 'col'), may hold values from -0.25 to 0.25
- query_bias: float32 [2, 512], P('pipe', 'col'), may hold values from -3 to 3
- value_bias: float32 [2, 512], P('pipe', 'col'), may hold values from -1.75 to 1.75
- proj_weight: bfloat16 [2, 512, 512], P('pipe', 'col', 'row'), may hold values from -1 to 1
- proj_bias: float32 [2, 512], P('pipe'), may hold values from -1.75 to 1.75
- second_gain: float32 [2, 512], P('pipe'), may hold values from 0.5 to 1.5
- second_shift: float32 [2, 512], P('pipe'), may hold values from -1.75 to 1.75
- up_weight: bfloat16 [2, 512, 2048], P('pipe', 'row', 'col'), may hold values from -0.25 to 0.25
- up_bias: float32 [2, 2048], P('pipe', 'col'), may hold values from -3 to 3
- down_weight: bfloat16 [2, 2048, 512], P('pipe', 'col', 'row'), may hold values from -0.125 to 0.125
- down_bias: float32 [2, 512], P('pipe'), may hold values from -1.75 to 1.75
- cotangent: bfloat16 [4, 8, 1024, 512], P(None, 'row', 'col'), may hold values from -6 to 6
- live_clips: int32 [4, 8], P(None, 'row'), may hold values 0 or 1
Outputs:
- states: bfloat16 [2, 4, 8, 1024, 512], P('pipe', None, 'row', 'col')
- state_grads: float32 [2, 4, 8, 1024, 512], P('pipe', None, 'row', 'col')
- grad_first_gain: float32 [2, 512], P('pipe')
- grad_first_shift: float32 [2, 512], P('pipe')
- grad_qkv_weight: float32 [2, 3, 512, 512], P('pipe', None, 'row', 'col')
- grad_query_bias: float32 [2, 512], P('pipe', 'col')
- grad_value_bias: float32 [2, 512], P('pipe', 'col')
- grad_proj_weight: float32 [2, 512, 512], P('pipe', 'col', 'row')
- grad_proj_bias: float32 [2, 512], P('pipe')
- grad_second_gain: float32 [2, 512], P('pipe')
- grad_second_shift: float32 [2, 512], P('pipe')
- grad_up_weight: float32 [2, 512, 2048], P('pipe', 'row', 'col')
- grad_up_bias: float32 [2, 2048], P('pipe', 'col')
- grad_down_weight: float32 [2, 2048, 512], P('pipe', 'col', 'row')
- grad_down_bias: float32 [2, 512], P('pipe')
All inputs are finite; a program needn't handle non-finite values. No bound on the sum of `live_clips` on one device may be relied on, other than what follows from the above.
Results may differ from a plain program's by a relative error of at most 0.015.
Values may be sent and summed in bfloat16 or wider, within the bound.
A program may use at most 192 MiB of HBM per device.

v0:
```python
import math
import jax
import jax.numpy as jnp
from jax import lax
from jax.sharding import PartitionSpec as P

HD = 64
epsilon = 1e-05


def from_behind(value, axis, steps):
    count = lax.axis_size(axis)
    first, last = (max(0, -steps), min(count, count - steps))
    return lax.ppermute(value, axis, [(source, source + steps) for source in range(first, last)])


def exact_gelu(values):
    return jax.nn.gelu(values, approximate=False)


def spread_features(normed):
    return lax.all_gather(normed, "col", axis=0, tiled=True)


def sum_columns(partial_rows):
    return lax.psum_scatter(partial_rows, "col", scatter_dimension=0, tiled=True)


def spread_grads(grad_low):
    return lax.all_gather(grad_low, "col", axis=0, tiled=True)


def sum_grad_columns(partial_rows):
    return lax.psum_scatter(partial_rows, "col", scatter_dimension=0, tiled=True)


def norm_forward(values, gain, shift):
    row_mean = jnp.mean(values, axis=-1, keepdims=True)
    row_var = jnp.mean(jnp.square(values - row_mean), axis=-1, keepdims=True)
    inv_std = lax.rsqrt(row_var + epsilon)
    centered = (values - row_mean) * inv_std
    return (centered, inv_std[:, 0], (centered * gain + shift).astype(jnp.bfloat16))


def norm_backward(grad_norm, centered, inv_std, gain):
    grad_gain = jnp.sum(grad_norm * centered, axis=0)
    grad_shift = jnp.sum(grad_norm, axis=0)
    scaled = grad_norm * gain
    first = jnp.mean(scaled, axis=-1, keepdims=True)
    second = jnp.mean(scaled * centered, axis=-1, keepdims=True)
    grad_in = inv_std[:, None] * (scaled - first - centered * second)
    return (grad_in, grad_gain, grad_shift)


def attention_probs(query_heads, key_heads):
    score_scale = 1.0 / math.sqrt(HD)
    scores = (
        jnp.einsum("qhd,khd->hqk", query_heads, key_heads, preferred_element_type=jnp.float32)
        * score_scale
    )
    return jax.nn.softmax(scores, axis=-1)


def layer_forward(values, weights, params):
    qkv_full, proj_full, up_full, down_full = weights
    (
        gain_one,
        shift_one,
        query_bias,
        value_bias,
        proj_bias,
        gain_two,
        shift_two,
        up_bias,
        down_bias,
    ) = params
    head_count = qkv_full.shape[2] // HD
    centered_one, inv_one, normed_one = norm_forward(values, gain_one, shift_one)
    attn_input = spread_features(normed_one)
    frame_count = attn_input.shape[0]
    projected = jnp.einsum("sd,jde->jse", attn_input, qkv_full, preferred_element_type=jnp.float32)
    query_heads = (
        (projected[0] + query_bias).astype(jnp.bfloat16).reshape(frame_count, head_count, HD)
    )
    key_heads = projected[1].astype(jnp.bfloat16).reshape(frame_count, head_count, HD)
    value_heads = (
        (projected[2] + value_bias).astype(jnp.bfloat16).reshape(frame_count, head_count, HD)
    )
    softmax_out = attention_probs(query_heads, key_heads)
    context = jnp.einsum(
        "hqk,khd->qhd",
        softmax_out.astype(jnp.bfloat16),
        value_heads,
        preferred_element_type=jnp.float32,
    )
    context = context.reshape(frame_count, head_count * HD).astype(jnp.bfloat16)
    attended = (
        sum_columns(jnp.dot(context, proj_full, preferred_element_type=jnp.float32)) + proj_bias
    )
    hidden = values + attended
    centered_two, inv_two, normed_two = norm_forward(hidden, gain_two, shift_two)
    mlp_input = spread_features(normed_two)
    pre_act = jnp.dot(mlp_input, up_full, preferred_element_type=jnp.float32) + up_bias
    activated = exact_gelu(pre_act).astype(jnp.bfloat16)
    output = (
        hidden
        + sum_columns(jnp.dot(activated, down_full, preferred_element_type=jnp.float32))
        + down_bias
    )
    kept = (
        centered_one,
        inv_one,
        attn_input,
        query_heads,
        key_heads,
        value_heads,
        context,
        centered_two,
        inv_two,
        mlp_input,
        pre_act,
        activated,
    )
    return (output, kept)


def layer_backward(grad_out, kept, weights, params):
    qkv_full, proj_full, up_full, down_full = weights
    (
        gain_one,
        shift_one,
        query_bias,
        value_bias,
        proj_bias,
        gain_two,
        shift_two,
        up_bias,
        down_bias,
    ) = params
    (
        centered_one,
        inv_one,
        attn_input,
        query_heads,
        key_heads,
        value_heads,
        context,
        centered_two,
        inv_two,
        mlp_input,
        pre_act,
        activated,
    ) = kept
    frame_count = attn_input.shape[0]
    score_scale = 1.0 / math.sqrt(HD)
    grad_down_bias = jnp.sum(grad_out, axis=0)
    down_grad = spread_grads(grad_out.astype(jnp.bfloat16))
    grad_down = jnp.einsum("sf,sd->fd", activated, down_grad, preferred_element_type=jnp.float32)
    grad_act = jnp.einsum("sd,fd->sf", down_grad, down_full, preferred_element_type=jnp.float32)
    unused, gelu_pull = jax.vjp(exact_gelu, pre_act)
    grad_pre = gelu_pull(grad_act)[0]
    grad_up_bias = jnp.sum(grad_pre, axis=0)
    grad_pre_low = grad_pre.astype(jnp.bfloat16)
    grad_up = jnp.einsum("sd,sf->df", mlp_input, grad_pre_low, preferred_element_type=jnp.float32)
    grad_normed_two = sum_grad_columns(
        jnp.einsum("sf,df->sd", grad_pre_low, up_full, preferred_element_type=jnp.float32)
    )
    grad_hidden_norm, grad_gain_two, grad_shift_two = norm_backward(
        grad_normed_two, centered_two, inv_two, gain_two
    )
    grad_hidden = grad_out + grad_hidden_norm
    grad_proj_bias = jnp.sum(grad_hidden, axis=0)
    proj_grad = spread_grads(grad_hidden.astype(jnp.bfloat16))
    grad_proj = jnp.einsum("se,sd->ed", context, proj_grad, preferred_element_type=jnp.float32)
    grad_context = jnp.einsum("sd,ed->se", proj_grad, proj_full, preferred_element_type=jnp.float32)
    grad_context = grad_context.astype(jnp.bfloat16).reshape(query_heads.shape)
    softmax_out = attention_probs(query_heads, key_heads)
    grad_probs = jnp.einsum(
        "qhd,khd->hqk", grad_context, value_heads, preferred_element_type=jnp.float32
    )
    grad_value = jnp.einsum(
        "hqk,qhd->khd",
        softmax_out.astype(jnp.bfloat16),
        grad_context,
        preferred_element_type=jnp.float32,
    )
    grad_scores = softmax_out * (
        grad_probs - jnp.sum(softmax_out * grad_probs, axis=-1, keepdims=True)
    )
    scores_low = grad_scores.astype(jnp.bfloat16)
    grad_query = (
        jnp.einsum("hqk,khd->qhd", scores_low, key_heads, preferred_element_type=jnp.float32)
        * score_scale
    )
    grad_key = (
        jnp.einsum("hqk,qhd->khd", scores_low, query_heads, preferred_element_type=jnp.float32)
        * score_scale
    )
    grad_query = grad_query.reshape(frame_count, -1)
    grad_key = grad_key.reshape(frame_count, -1)
    grad_value = grad_value.reshape(frame_count, -1)
    grad_query_bias = jnp.sum(grad_query, axis=0)
    grad_value_bias = jnp.sum(grad_value, axis=0)
    grad_qkv_low = jnp.stack([grad_query, grad_key, grad_value]).astype(jnp.bfloat16)
    grad_qkv = jnp.einsum(
        "sd,jse->jde", attn_input, grad_qkv_low, preferred_element_type=jnp.float32
    )
    grad_normed_one = sum_grad_columns(
        jnp.einsum("jse,jde->sd", grad_qkv_low, qkv_full, preferred_element_type=jnp.float32)
    )
    grad_in_norm, grad_gain_one, grad_shift_one = norm_backward(
        grad_normed_one, centered_one, inv_one, gain_one
    )
    grad_in = grad_hidden + grad_in_norm
    weight_grads = (grad_qkv, grad_proj, grad_up, grad_down)
    vector_grads = (
        grad_gain_one,
        grad_shift_one,
        grad_query_bias,
        grad_value_bias,
        grad_proj_bias,
        grad_gain_two,
        grad_shift_two,
        grad_up_bias,
        grad_down_bias,
    )
    return (grad_in, weight_grads, vector_grads)


def store_slot(buffer, slot_index, is_valid, value):
    current = lax.dynamic_index_in_dim(buffer, slot_index, 0, keepdims=False)
    return lax.dynamic_update_index_in_dim(
        buffer, jnp.where(is_valid, value, current), slot_index, 0
    )


def reduce_end(weight_acc):
    return (
        lax.psum_scatter(
            weight_acc[0].astype(jnp.bfloat16), "row", scatter_dimension=1, tiled=True
        ).astype(jnp.float32),
        lax.psum_scatter(
            weight_acc[1].astype(jnp.bfloat16), "row", scatter_dimension=1, tiled=True
        ).astype(jnp.float32),
        lax.psum_scatter(
            weight_acc[2].astype(jnp.bfloat16), "row", scatter_dimension=0, tiled=True
        ).astype(jnp.float32),
        lax.psum_scatter(
            weight_acc[3].astype(jnp.bfloat16), "row", scatter_dimension=1, tiled=True
        ).astype(jnp.float32),
    )


def on_device(
    inputs,
    first_gain,
    first_shift,
    qkv_weight,
    query_bias,
    value_bias,
    proj_weight,
    proj_bias,
    second_gain,
    second_shift,
    up_weight,
    up_bias,
    down_weight,
    down_bias,
    cotangent,
    live_clips,
):
    micro_count = inputs.shape[0]
    row_count = inputs.shape[2]
    feature_count = inputs.shape[3]
    section_index = lax.axis_index("pipe")
    weights = (
        lax.all_gather(qkv_weight[0], "row", axis=1, tiled=True),
        lax.all_gather(proj_weight[0], "row", axis=1, tiled=True),
        lax.all_gather(up_weight[0], "row", axis=0, tiled=True),
        lax.all_gather(down_weight[0], "row", axis=1, tiled=True),
    )
    params = (
        first_gain[0],
        first_shift[0],
        query_bias[0],
        value_bias[0],
        proj_bias[0],
        second_gain[0],
        second_shift[0],
        up_bias[0],
        down_bias[0],
    )
    kept_buffers = ()
    zero_rows = jnp.zeros((row_count, feature_count), jnp.bfloat16)
    zero_stack = jnp.zeros((micro_count, row_count, feature_count), jnp.bfloat16)
    own_inputs = inputs[:, 0]

    def forward_tick(state_carry, tick_index):
        received, outputs, layer_inputs, buffers = state_carry
        batch_index = tick_index - section_index
        is_valid = (batch_index >= 0) & (batch_index < micro_count)
        slot_index = jnp.clip(batch_index, 0, micro_count - 1)
        own_input = lax.dynamic_index_in_dim(
            own_inputs, jnp.minimum(tick_index, micro_count - 1), 0, keepdims=False
        )
        layer_input = jnp.where(section_index == 0, own_input, received)
        output, kept = layer_forward(layer_input.astype(jnp.float32), weights, params)
        output_low = output.astype(jnp.bfloat16)
        passed = from_behind(output_low, "pipe", 1)
        outputs = store_slot(outputs, slot_index, is_valid, output_low)
        layer_inputs = store_slot(layer_inputs, slot_index, is_valid, layer_input)
        return ((passed, outputs, layer_inputs, buffers), None)

    tick_range = jnp.arange(micro_count + 1)
    forward_out, unused = lax.scan(
        forward_tick, (zero_rows, zero_stack, zero_stack, kept_buffers), tick_range
    )
    unused_rows, outputs, layer_inputs, kept_buffers = forward_out
    weight_acc = tuple((jnp.zeros(part.shape, jnp.float32) for part in weights))
    vector_acc = tuple((jnp.zeros(part.shape, jnp.float32) for part in params))
    grads_init = jnp.zeros((micro_count, row_count, feature_count), jnp.float32)
    live_rows = live_clips[:, 0]
    cot_rows_all = cotangent[:, 0]

    def backward_tick(state_carry, tick_index):
        received, grads_in, weight_sum, vector_sum = state_carry
        batch_index = micro_count - tick_index - section_index
        is_valid = (batch_index >= 0) & (batch_index < micro_count)
        slot_index = jnp.clip(batch_index, 0, micro_count - 1)
        cot_rows = lax.dynamic_index_in_dim(cot_rows_all, slot_index, 0, keepdims=False).astype(
            jnp.float32
        )
        live_flag = lax.dynamic_index_in_dim(live_rows, slot_index, 0, keepdims=False).astype(
            jnp.float32
        )
        grad_out = jnp.where(
            section_index == 1, cot_rows * live_flag, received.astype(jnp.float32)
        ) * is_valid.astype(jnp.float32)
        stored_input = lax.dynamic_index_in_dim(layer_inputs, slot_index, 0, keepdims=False)
        kept = layer_forward(stored_input.astype(jnp.float32), weights, params)[1]
        grad_in, weight_grads, vector_grads = layer_backward(grad_out, kept, weights, params)
        passed = from_behind(grad_in.astype(jnp.bfloat16), "pipe", -1)
        grads_in = store_slot(grads_in, slot_index, is_valid, grad_in)
        weight_sum = jax.tree.map(jnp.add, weight_sum, weight_grads)
        vector_sum = jax.tree.map(jnp.add, vector_sum, vector_grads)
        return ((passed, grads_in, weight_sum, vector_sum), None)

    backward_out, unused_two = lax.scan(
        backward_tick, (zero_rows, grads_init, weight_acc, vector_acc), tick_range
    )
    unused_grad, grads_in, weight_acc, vector_acc = backward_out
    weight_out = reduce_end(weight_acc)
    split_out = lax.psum((vector_acc[2], vector_acc[3], vector_acc[7]), "row")
    whole_out = lax.psum(
        (vector_acc[0], vector_acc[1], vector_acc[4], vector_acc[5], vector_acc[6], vector_acc[8]),
        ("row", "col"),
    )
    return (
        outputs[None, :, None],
        grads_in[None, :, None],
        whole_out[0][None],
        whole_out[1][None],
        weight_out[0][None],
        split_out[0][None],
        split_out[1][None],
        weight_out[1][None],
        whole_out[2][None],
        whole_out[3][None],
        whole_out[4][None],
        weight_out[2][None],
        split_out[2][None],
        weight_out[3][None],
        whole_out[5][None],
    )


def solution(mesh):
    placed = (
        P(None, "row", "col", None),
        P("pipe", None),
        P("pipe", None),
        P("pipe", None, "row", "col"),
        P("pipe", "col"),
        P("pipe", "col"),
        P("pipe", "col", "row"),
        P("pipe", None),
        P("pipe", None),
        P("pipe", None),
        P("pipe", "row", "col"),
        P("pipe", "col"),
        P("pipe", "col", "row"),
        P("pipe", None),
        P(None, "row", "col", None),
        P(None, "row"),
    )
    return jax.shard_map(
        on_device,
        mesh=mesh,
        in_specs=placed,
        out_specs=(
            P("pipe", None, "row", "col", None),
            P("pipe", None, "row", "col", None),
            P("pipe", None),
            P("pipe", None),
            P("pipe", None, "row", "col"),
            P("pipe", "col"),
            P("pipe", "col"),
            P("pipe", "col", "row"),
            P("pipe", None),
            P("pipe", None),
            P("pipe", None),
            P("pipe", "row", "col"),
            P("pipe", "col"),
            P("pipe", "col", "row"),
            P("pipe", None),
        ),
        check_vma=False,
    )
```

profile of v0, /device:TPU:0, one launch (start us, length us, event | category | flops | bytes accessed | tf_op | source)
XLA Modules:
  0.0 2830.5 jit_solution(8740462381904181484)
XLA Ops:
  25.8 18.5 all-gather
  61.8 961.5 %while.55 = (s32[]{:T(128)}, bf16[512,512]{1,0:T(8,128)(2,1)S(1)}, bf16[4,512,512]{2,1,0:T(8,128)(2,1)}, bf16[4,512,512]{2,1,0:T(8,128)(2,1)}, pred[]{:T(512)}, ...) while((s32[]{:T(128)}, bf16[512,512]{1,0:T(8,128)(2,1)S(1)}, ...), condition=%wide.region_9.10_spmd, body=%wide.region_0.9_spmd.sunk | while | flops 4413463552 | bytes 122786912 | solution.py:315
  70.8 19.0 all-gather.17.cloned.1.call-done
  131.7 31.9 %reduce-scatter.18.cloned.1.call-done = f32[512,512]{1,0:T(8,128)} async-done(((f32[1024,512]{1,0:T(8,128)}), f32[512,512]{1,0:T(8,128)}) %reduce-scatter.18.cloned.1.call-update) | async-done | bytes 1048592 | tf_op jit(solution)/shard_map/while/body/eval_jaxpr/reduce_scatter | solution.py:26
  169.0 21.4 all-gather.19.cloned.1.call-done
  205.1 30.9 %reduce-scatter.20.cloned.1.call-done = f32[512,512]{1,0:T(8,128)} async-done(((f32[1024,512]{1,0:T(8,128)}), f32[512,512]{1,0:T(8,128)}) %reduce-scatter.20.cloned.1.call-update) | async-done | bytes 1048592 | tf_op jit(solution)/shard_map/while/body/eval_jaxpr/reduce_scatter | solution.py:26
  262.0 20.3 all-gather.17.cloned.1.call-done
  324.3 31.9 %reduce-scatter.18.cloned.1.call-done = f32[512,512]{1,0:T(8,128)} async-done(((f32[1024,512]{1,0:T(8,128)}), f32[512,512]{1,0:T(8,128)}) %reduce-scatter.18.cloned.1.call-update) | async-done | bytes 1048592 | tf_op jit(solution)/shard_map/while/body/eval_jaxpr/reduce_scatter | solution.py:26
  361.6 21.4 all-gather.19.cloned.1.call-done
  397.6 30.9 %reduce-scatter.20.cloned.1.call-done = f32[512,512]{1,0:T(8,128)} async-done(((f32[1024,512]{1,0:T(8,128)}), f32[512,512]{1,0:T(8,128)}) %reduce-scatter.20.cloned.1.call-update) | async-done | bytes 1048592 | tf_op jit(solution)/shard_map/while/body/eval_jaxpr/reduce_scatter | solution.py:26
  454.5 20.3 all-gather.17.cloned.1.call-done
  516.7 31.9 %reduce-scatter.18.cloned.1.call-done = f32[512,512]{1,0:T(8,128)} async-done(((f32[1024,512]{1,0:T(8,128)}), f32[512,512]{1,0:T(8,128)}) %reduce-scatter.18.cloned.1.call-update) | async-done | bytes 1048592 | tf_op jit(solution)/shard_map/while/body/eval_jaxpr/reduce_scatter | solution.py:26
  554.0 21.4 all-gather.19.cloned.1.call-done
  590.1 30.9 %reduce-scatter.20.cloned.1.call-done = f32[512,512]{1,0:T(8,128)} async-done(((f32[1024,512]{1,0:T(8,128)}), f32[512,512]{1,0:T(8,128)}) %reduce-scatter.20.cloned.1.call-update) | async-done | bytes 1048592 | tf_op jit(solution)/shard_map/while/body/eval_jaxpr/reduce_scatter | solution.py:26
  647.0 20.3 all-gather.17.cloned.1.call-done
  709.2 31.9 %reduce-scatter.18.cloned.1.call-done = f32[512,512]{1,0:T(8,128)} async-done(((f32[1024,512]{1,0:T(8,128)}), f32[512,512]{1,0:T(8,128)}) %reduce-scatter.18.cloned.1.call-update) | async-done | bytes 1048592 | tf_op jit(solution)/shard_map/while/body/eval_jaxpr/reduce_scatter | solution.py:26
  746.5 21.4 all-gather.19.cloned.1.call-done
  782.6 30.9 %reduce-scatter.20.cloned.1.call-done = f32[512,512]{1,0:T(8,128)} async-done(((f32[1024,512]{1,0:T(8,128)}), f32[512,512]{1,0:T(8,128)}) %reduce-scatter.20.cloned.1.call-update) | async-done | bytes 1048592 | tf_op jit(solution)/shard_map/while/body/eval_jaxpr/reduce_scatter | solution.py:26
  839.5 20.3 all-gather.17.cloned.1.call-done
  901.7 31.9 %reduce-scatter.18.cloned.1.call-done = f32[512,512]{1,0:T(8,128)} async-done(((f32[1024,512]{1,0:T(8,128)}), f32[512,512]{1,0:T(8,128)}) %reduce-scatter.18.cloned.1.call-update) | async-done | bytes 1048592 | tf_op jit(solution)/shard_map/while/body/eval_jaxpr/reduce_scatter | solution.py:26
  939.0 21.4 all-gather.19.cloned.1.call-done
  975.1 30.9 %reduce-scatter.20.cloned.1.call-done = f32[512,512]{1,0:T(8,128)} async-done(((f32[1024,512]{1,0:T(8,128)}), f32[512,512]{1,0:T(8,128)}) %reduce-scatter.20.cloned.1.call-update) | async-done | bytes 1048592 | tf_op jit(solution)/shard_map/while/body/eval_jaxpr/reduce_scatter | solution.py:26
  1027.3 1663.7 %while.56 = (s32[]{:T(128)}, bf16[512,512]{1,0:T(8,128)(2,1)}, f32[4,512,512]{2,1,0:T(8,128)}, f32[3,512,256]{1,2,0:T(8,128)}, f32[256,512]{1,0:T(8,128)}, /*ind...) while((s32[]{:T(128)}, bf16[512,512]{1,0:T(8,128)(2,1)}, ...), condition=%wide.region_34.35_spmd.clone, body=%wide.region_10.34_spmd.clone.sunk | while | flops 12016956416 | bytes 501957632 | solution.py:348
  1059.1 20.3 all-gather.21.cloned.1.call-done
  1091.0 19.1 fusion.289
  1129.0 31.9 %reduce-scatter.22.cloned.1.call-done = f32[512,512]{1,0:T(8,128)} async-done(((f32[1024,512]{1,0:T(8,128)}), f32[512,512]{1,0:T(8,128)}) %reduce-scatter.22.cloned.1.call-update) | async-done | bytes 1048592 | tf_op jit(solution)/shard_map/while/body/eval_jaxpr/reduce_scatter | solution.py:26
  1168.0 17.2 all-gather.23.cloned.1.call-done
  1218.2 31.9 %reduce-scatter.24.cloned.1.call-done = f32[512,512]{1,0:T(8,128)} async-done(((f32[1024,512]{1,0:T(8,128)}), f32[512,512]{1,0:T(8,128)}) %reduce-scatter.24.cloned.1.call-update) | async-done | bytes 1048592 | tf_op jit(solution)/shard_map/while/body/eval_jaxpr/reduce_scatter | solution.py:34
  1256.2 21.4 all-gather.27.cloned.1.call-done
  1293.7 16.5 multiply_reduce_fusion.16
  1340.6 18.1 reduce-scatter.26.cloned.1.call-done
  1388.8 18.5 all-gather.21.cloned.1.call-done
  1418.8 19.1 fusion.289
  1456.8 31.9 %reduce-scatter.22.cloned.1.call-done = f32[512,512]{1,0:T(8,128)} async-done(((f32[1024,512]{1,0:T(8,128)}), f32[512,512]{1,0:T(8,128)}) %reduce-scatter.22.cloned.1.call-update) | async-done | bytes 1048592 | tf_op jit(solution)/shard_map/while/body/eval_jaxpr/reduce_scatter | solution.py:26
  1495.8 17.2 all-gather.23.cloned.1.call-done
  1546.0 31.9 %reduce-scatter.24.cloned.1.call-done = f32[512,512]{1,0:T(8,128)} async-done(((f32[1024,512]{1,0:T(8,128)}), f32[512,512]{1,0:T(8,128)}) %reduce-scatter.24.cloned.1.call-update) | async-done | bytes 1048592 | tf_op jit(solution)/shard_map/while/body/eval_jaxpr/reduce_scatter | solution.py:34
  1584.0 21.4 all-gather.27.cloned.1.call-done
  1621.5 16.5 multiply_reduce_fusion.16
  1669.6 17.0 reduce-scatter.26.cloned.1.call-done
  1716.5 18.5 all-gather.21.cloned.1.call-done
  1746.6 19.1 fusion.289
  1784.6 31.9 %reduce-scatter.22.cloned.1.call-done = f32[512,512]{1,0:T(8,128)} async-done(((f32[1024,512]{1,0:T(8,128)}), f32[512,512]{1,0:T(8,128)}) %reduce-scatter.22.cloned.1.call-update) | async-done | bytes 1048592 | tf_op jit(solution)/shard_map/while/body/eval_jaxpr/reduce_scatter | solution.py:26
  1823.6 17.2 all-gather.23.cloned.1.call-done
  1874.0 31.9 %reduce-scatter.24.cloned.1.call-done = f32[512,512]{1,0:T(8,128)} async-done(((f32[1024,512]{1,0:T(8,128)}), f32[512,512]{1,0:T(8,128)}) %reduce-scatter.24.cloned.1.call-update) | async-done | bytes 1048592 | tf_op jit(solution)/shard_map/while/body/eval_jaxpr/reduce_scatter | solution.py:34
  1911.9 21.4 all-gather.27.cloned.1.call-done
  1949.4 16.5 multiply_reduce_fusion.16
  1997.5 17.0 reduce-scatter.26.cloned.1.call-done
  2044.5 18.5 all-gather.21.cloned.1.call-done
  2074.5 19.1 fusion.289
  2112.5 31.9 %reduce-scatter.22.cloned.1.call-done = f32[512,512]{1,0:T(8,128)} async-done(((f32[1024,512]{1,0:T(8,128)}), f32[512,512]{1,0:T(8,128)}) %reduce-scatter.22.cloned.1.call-update) | async-done | bytes 1048592 | tf_op jit(solution)/shard_map/while/body/eval_jaxpr/reduce_scatter | solution.py:26
  2151.6 17.2 all-gather.23.cloned.1.call-done
  2201.8 31.9 %reduce-scatter.24.cloned.1.call-done = f32[512,512]{1,0:T(8,128)} async-done(((f32[1024,512]{1,0:T(8,128)}), f32[512,512]{1,0:T(8,128)}) %reduce-scatter.24.cloned.1.call-update) | async-done | bytes 1048592 | tf_op jit(solution)/shard_map/while/body/eval_jaxpr/reduce_scatter | solution.py:34
  2239.7 21.4 all-gather.27.cloned.1.call-done
  2325.3 17.0 reduce-scatter.26.cloned.1.call-done
  2372.3 18.5 all-gather.21.cloned.1.call-done
  2402.4 19.1 fusion.289
  2440.3 31.9 %reduce-scatter.22.cloned.1.call-done = f32[512,512]{1,0:T(8,128)} async-done(((f32[1024,512]{1,0:T(8,128)}), f32[512,512]{1,0:T(8,128)}) %reduce-scatter.22.cloned.1.call-update) | async-done | bytes 1048592 | tf_op jit(solution)/shard_map/while/body/eval_jaxpr/reduce_scatter | solution.py:26
  2479.4 17.2 all-gather.23.cloned.1.call-done
  2529.8 31.9 %reduce-scatter.24.cloned.1.call-done = f32[512,512]{1,0:T(8,128)} async-done(((f32[1024,512]{1,0:T(8,128)}), f32[512,512]{1,0:T(8,128)}) %reduce-scatter.24.cloned.1.call-update) | async-done | bytes 1048592 | tf_op jit(solution)/shard_map/while/body/eval_jaxpr/reduce_scatter | solution.py:34
  2567.7 21.4 all-gather.27.cloned.1.call-done
  2605.2 16.5 multiply_reduce_fusion.16
  2653.3 17.0 reduce-scatter.26.cloned.1.call-done
  2716.6 58.3 %all-reduce = (f32[1,512]{1,0:T(1,128)}, f32[1,512]{1,0:T(1,128)}, f32[1,512]{1,0:T(1,128)}, f32[1,512]{1,0:T(1,128)}, f32[1,512]{1,0:T(1,128)}, /*index=5*/f32[1,512]{1,0:T(1,128)}) all-reduce(f32[1,512]{1,0:T(1,128)S(1)} %bitcast.384, f32[1,512]{1,0:T(1,128)S(1)} %bitcast.383, ...), channel_id=1, replica_groups=mesh['pipe'=2,'row'=8,'col'=2] {'row','col'}, use_global_device_ids=true, to_apply=%region_35.36 | all-reduce | flops 3072 | bytes 24576 | tf_op jit(solution)/shard_map/psum | solution.py:354
  2790.4 31.3 %reduce-scatter.16.cloned.1.call-done = bf16[1024,64]{0,1:T(8,128)(2,1)} async-done(((bf16[1024,512]{0,1:T(8,128)(2,1)}), bf16[1024,64]{0,1:T(8,128)(2,1)}) %reduce-scatter.16.cloned.1.call-update) | async-done | bytes 131088 | tf_op jit(solution)/shard_map/reduce_scatter | solution.py:248
  (1363 shorter events, 1289.6 us)
Async XLA Ops:
  7.2 38.7 %all-gather.15.cloned.1.call-start = ((), (), s32[]{:S(2)}) async-start(), calls=%async_computation.14 | async-start | bytes 1179648 | tf_op jit(solution)/shard_map/all_gather | solution.py:280
  7.9 50.9 %all-gather.13.cloned.1.call-start = ((), (), s32[]{:S(2)}) async-start(), calls=%async_computation.13 | async-start | bytes 1179648 | tf_op jit(solution)/shard_map/all_gather | solution.py:279
  62.1 27.8 all-gather.17.cloned.1.call-start
  68.8 94.9 %reduce-scatter.18.cloned.1.call-start = ((), (), s32[]{:S(2)}) async-start(), calls=%async_computation.16 | async-start | bytes 3145728 | tf_op jit(solution)/shard_map/while/body/eval_jaxpr/reduce_scatter | solution.py:26
  131.7 58.8 %all-gather.19.cloned.1.call-start = ((), (), s32[]{:S(2)}) async-start(), calls=%async_computation.17 | async-start | bytes 1572864 | tf_op jit(solution)/shard_map/while/body/eval_jaxpr/all_gather | solution.py:22
  169.0 67.0 %reduce-scatter.20.cloned.1.call-start = ((), (), s32[]{:S(2)}) async-start(), calls=%async_computation.18 | async-start | bytes 3145728 | tf_op jit(solution)/shard_map/while/body/eval_jaxpr/reduce_scatter | solution.py:26
  253.3 29.0 %all-gather.17.cloned.1.call-start = ((), (), s32[]{:S(2)}) async-start(), calls=%async_computation.15 | async-start | bytes 1572864 | tf_op jit(solution)/shard_map/while/body/eval_jaxpr/all_gather | solution.py:22
  260.0 96.2 %reduce-scatter.18.cloned.1.call-start = ((), (), s32[]{:S(2)}) async-start(), calls=%async_computation.16 | async-start | bytes 3145728 | tf_op jit(solution)/shard_map/while/body/eval_jaxpr/reduce_scatter | solution.py:26
  324.2 58.8 %all-gather.19.cloned.1.call-start = ((), (), s32[]{:S(2)}) async-start(), calls=%async_computation.17 | async-start | bytes 1572864 | tf_op jit(solution)/shard_map/while/body/eval_jaxpr/all_gather | solution.py:22
  361.5 67.0 %reduce-scatter.20.cloned.1.call-start = ((), (), s32[]{:S(2)}) async-start(), calls=%async_computation.18 | async-start | bytes 3145728 | tf_op jit(solution)/shard_map/while/body/eval_jaxpr/reduce_scatter | solution.py:26
  445.8 29.0 %all-gather.17.cloned.1.call-start = ((), (), s32[]{:S(2)}) async-start(), calls=%async_computation.15 | async-start | bytes 1572864 | tf_op jit(solution)/shard_map/while/body/eval_jaxpr/all_gather | solution.py:22
  452.5 96.2 %reduce-scatter.18.cloned.1.call-start = ((), (), s32[]{:S(2)}) async-start(), calls=%async_computation.16 | async-start | bytes 3145728 | tf_op jit(solution)/shard_map/while/body/eval_jaxpr/reduce_scatter | solution.py:26
  516.7 58.8 %all-gather.19.cloned.1.call-start = ((), (), s32[]{:S(2)}) async-start(), calls=%async_computation.17 | async-start | bytes 1572864 | tf_op jit(solution)/shard_map/while/body/eval_jaxpr/all_gather | solution.py:22
  554.0 67.0 %reduce-scatter.20.cloned.1.call-start = ((), (), s32[]{:S(2)}) async-start(), calls=%async_computation.18 | async-start | bytes 3145728 | tf_op jit(solution)/shard_map/while/body/eval_jaxpr/reduce_scatter | solution.py:26
  638.3 29.0 %all-gather.17.cloned.1.call-start = ((), (), s32[]{:S(2)}) async-start(), calls=%async_computation.15 | async-start | bytes 1572864 | tf_op jit(solution)/shard_map/while/body/eval_jaxpr/all_gather | solution.py:22
  645.0 96.2 %reduce-scatter.18.cloned.1.call-start = ((), (), s32[]{:S(2)}) async-start(), calls=%async_computation.16 | async-start | bytes 3145728 | tf_op jit(solution)/shard_map/while/body/eval_jaxpr/reduce_scatter | solution.py:26
  709.2 58.8 %all-gather.19.cloned.1.call-start = ((), (), s32[]{:S(2)}) async-start(), calls=%async_computation.17 | async-start | bytes 1572864 | tf_op jit(solution)/shard_map/while/body/eval_jaxpr/all_gather | solution.py:22
  746.5 67.0 %reduce-scatter.20.cloned.1.call-start = ((), (), s32[]{:S(2)}) async-start(), calls=%async_computation.18 | async-start | bytes 3145728 | tf_op jit(solution)/shard_map/while/body/eval_jaxpr/reduce_scatter | solution.py:26
  830.8 29.0 %all-gather.17.cloned.1.call-start = ((), (), s32[]{:S(2)}) async-start(), calls=%async_computation.15 | async-start | bytes 1572864 | tf_op jit(solution)/shard_map/while/body/eval_jaxpr/all_gather | solution.py:22
  837.5 96.2 %reduce-scatter.18.cloned.1.call-start = ((), (), s32[]{:S(2)}) async-start(), calls=%async_computation.16 | async-start | bytes 3145728 | tf_op jit(solution)/shard_map/while/body/eval_jaxpr/reduce_scatter | solution.py:26
  901.7 58.8 %all-gather.19.cloned.1.call-start = ((), (), s32[]{:S(2)}) async-start(), calls=%async_computation.17 | async-start | bytes 1572864 | tf_op jit(solution)/shard_map/while/body/eval_jaxpr/all_gather | solution.py:22
  939.0 67.0 %reduce-scatter.20.cloned.1.call-start = ((), (), s32[]{:S(2)}) async-start(), calls=%async_computation.18 | async-start | bytes 3145728 | tf_op jit(solution)/shard_map/while/body/eval_jaxpr/reduce_scatter | solution.py:26
  1049.8 29.6 %all-gather.21.cloned.1.call-start = ((), (), s32[]{:S(2)}) async-start(), calls=%async_computation.19 | async-start | bytes 1572864 | tf_op jit(solution)/shard_map/while/body/eval_jaxpr/all_gather | solution.py:22
  1057.0 103.8 %reduce-scatter.22.cloned.1.call-start = ((), (), s32[]{:S(2)}) async-start(), calls=%async_computation.20 | async-start | bytes 3145728 | tf_op jit(solution)/shard_map/while/body/eval_jaxpr/reduce_scatter | solution.py:26
  1128.9 56.3 %all-gather.23.cloned.1.call-start = ((), (), s32[]{:S(2)}) async-start(), calls=%async_computation.21 | async-start | bytes 1572864 | tf_op jit(solution)/shard_map/while/body/eval_jaxpr/all_gather | solution.py:22
  1163.8 44.3 %all-gather.25.cloned.1.call-start = ((), (), s32[]{:S(2)}) async-start(), calls=%async_computation.22 | async-start | bytes 1572864 | tf_op jit(solution)/shard_map/while/body/eval_jaxpr/all_gather | solution.py:30
  1168.0 82.2 %reduce-scatter.24.cloned.1.call-start = ((), (), s32[]{:S(2)}) async-start(), calls=%async_computation.23 | async-start | bytes 3145728 | tf_op jit(solution)/shard_map/while/body/eval_jaxpr/reduce_scatter | solution.py:34
  1218.2 59.4 %all-gather.27.cloned.1.call-start = ((), (), s32[]{:S(2)}) async-start(), calls=%async_computation.24 | async-start | bytes 1572864 | tf_op jit(solution)/shard_map/while/body/eval_jaxpr/all_gather | solution.py:30
  1256.1 102.7 %reduce-scatter.26.cloned.1.call-start = ((), (), s32[]{:S(2)}) async-start(), calls=%async_computation.25 | async-start | bytes 3145728 | tf_op jit(solution)/shard_map/while/body/eval_jaxpr/reduce_scatter | solution.py:34
  1363.7 15.7 collective-permute-start.1
  1379.5 27.8 all-gather.21.cloned.1.call-start
  1386.7 102.0 %reduce-scatter.22.cloned.1.call-start = ((), (), s32[]{:S(2)}) async-start(), calls=%async_computation.20 | async-start | bytes 3145728 | tf_op jit(solution)/shard_map/while/body/eval_jaxpr/reduce_scatter | solution.py:26
  1456.7 56.3 %all-gather.23.cloned.1.call-start = ((), (), s32[]{:S(2)}) async-start(), calls=%async_computation.21 | async-start | bytes 1572864 | tf_op jit(solution)/shard_map/while/body/eval_jaxpr/all_gather | solution.py:22
  1491.6 44.3 %all-gather.25.cloned.1.call-start = ((), (), s32[]{:S(2)}) async-start(), calls=%async_computation.22 | async-start | bytes 1572864 | tf_op jit(solution)/shard_map/while/body/eval_jaxpr/all_gather | solution.py:30
  1495.8 82.2 %reduce-scatter.24.cloned.1.call-start = ((), (), s32[]{:S(2)}) async-start(), calls=%async_computation.23 | async-start | bytes 3145728 | tf_op jit(solution)/shard_map/while/body/eval_jaxpr/reduce_scatter | solution.py:34
  1546.0 59.4 %all-gather.27.cloned.1.call-start = ((), (), s32[]{:S(2)}) async-start(), calls=%async_computation.24 | async-start | bytes 1572864 | tf_op jit(solution)/shard_map/while/body/eval_jaxpr/all_gather | solution.py:30
  1583.9 102.7 %reduce-scatter.26.cloned.1.call-start = ((), (), s32[]{:S(2)}) async-start(), calls=%async_computation.25 | async-start | bytes 3145728 | tf_op jit(solution)/shard_map/while/body/eval_jaxpr/reduce_scatter | solution.py:34
  1691.5 15.7 collective-permute-start.1
  1707.3 27.8 all-gather.21.cloned.1.call-start
  1714.5 102.0 %reduce-scatter.22.cloned.1.call-start = ((), (), s32[]{:S(2)}) async-start(), calls=%async_computation.20 | async-start | bytes 3145728 | tf_op jit(solution)/shard_map/while/body/eval_jaxpr/reduce_scatter | solution.py:26
  1784.5 56.3 %all-gather.23.cloned.1.call-start = ((), (), s32[]{:S(2)}) async-start(), calls=%async_computation.21 | async-start | bytes 1572864 | tf_op jit(solution)/shard_map/while/body/eval_jaxpr/all_gather | solution.py:22
  1819.4 44.4 %all-gather.25.cloned.1.call-start = ((), (), s32[]{:S(2)}) async-start(), calls=%async_computation.22 | async-start | bytes 1572864 | tf_op jit(solution)/shard_map/while/body/eval_jaxpr/all_gather | solution.py:30
  1823.6 82.3 %reduce-scatter.24.cloned.1.call-start = ((), (), s32[]{:S(2)}) async-start(), calls=%async_computation.23 | async-start | bytes 3145728 | tf_op jit(solution)/shard_map/while/body/eval_jaxpr/reduce_scatter | solution.py:34
  1873.9 59.4 %all-gather.27.cloned.1.call-start = ((), (), s32[]{:S(2)}) async-start(), calls=%async_computation.24 | async-start | bytes 1572864 | tf_op jit(solution)/shard_map/while/body/eval_jaxpr/all_gather | solution.py:30
  1911.9 102.7 %reduce-scatter.26.cloned.1.call-start = ((), (), s32[]{:S(2)}) async-start(), calls=%async_computation.25 | async-start | bytes 3145728 | tf_op jit(solution)/shard_map/while/body/eval_jaxpr/reduce_scatter | solution.py:34
  2019.5 15.7 collective-permute-start.1
  2035.2 27.8 all-gather.21.cloned.1.call-start
  2042.4 102.0 %reduce-scatter.22.cloned.1.call-start = ((), (), s32[]{:S(2)}) async-start(), calls=%async_computation.20 | async-start | bytes 3145728 | tf_op jit(solution)/shard_map/while/body/eval_jaxpr/reduce_scatter | solution.py:26
  2112.5 56.3 %all-gather.23.cloned.1.call-start = ((), (), s32[]{:S(2)}) async-start(), calls=%async_computation.21 | async-start | bytes 1572864 | tf_op jit(solution)/shard_map/while/body/eval_jaxpr/all_gather | solution.py:22
  2147.4 44.3 %all-gather.25.cloned.1.call-start = ((), (), s32[]{:S(2)}) async-start(), calls=%async_computation.22 | async-start | bytes 1572864 | tf_op jit(solution)/shard_map/while/body/eval_jaxpr/all_gather | solution.py:30
  2151.5 82.2 %reduce-scatter.24.cloned.1.call-start = ((), (), s32[]{:S(2)}) async-start(), calls=%async_computation.23 | async-start | bytes 3145728 | tf_op jit(solution)/shard_map/while/body/eval_jaxpr/reduce_scatter | solution.py:34
  2201.7 59.4 %all-gather.27.cloned.1.call-start = ((), (), s32[]{:S(2)}) async-start(), calls=%async_computation.24 | async-start | bytes 1572864 | tf_op jit(solution)/shard_map/while/body/eval_jaxpr/all_gather | solution.py:30
  2239.7 102.7 %reduce-scatter.26.cloned.1.call-start = ((), (), s32[]{:S(2)}) async-start(), calls=%async_computation.25 | async-start | bytes 3145728 | tf_op jit(solution)/shard_map/while/body/eval_jaxpr/reduce_scatter | solution.py:34
  2363.1 27.8 all-gather.21.cloned.1.call-start
  2370.3 102.0 %reduce-scatter.22.cloned.1.call-start = ((), (), s32[]{:S(2)}) async-start(), calls=%async_computation.20 | async-start | bytes 3145728 | tf_op jit(solution)/shard_map/while/body/eval_jaxpr/reduce_scatter | solution.py:26
  2440.3 56.3 %all-gather.23.cloned.1.call-start = ((), (), s32[]{:S(2)}) async-start(), calls=%async_computation.21 | async-start | bytes 1572864 | tf_op jit(solution)/shard_map/while/body/eval_jaxpr/all_gather | solution.py:22
  2475.2 44.4 %all-gather.25.cloned.1.call-start = ((), (), s32[]{:S(2)}) async-start(), calls=%async_computation.22 | async-start | bytes 1572864 | tf_op jit(solution)/shard_map/while/body/eval_jaxpr/all_gather | solution.py:30
  2479.3 82.3 %reduce-scatter.24.cloned.1.call-start = ((), (), s32[]{:S(2)}) async-start(), calls=%async_computation.23 | async-start | bytes 3145728 | tf_op jit(solution)/shard_map/while/body/eval_jaxpr/reduce_scatter | solution.py:34
  2529.7 59.4 %all-gather.27.cloned.1.call-start = ((), (), s32[]{:S(2)}) async-start(), calls=%async_computation.24 | async-start | bytes 1572864 | tf_op jit(solution)/shard_map/while/body/eval_jaxpr/all_gather | solution.py:30
  2567.6 102.7 %reduce-scatter.26.cloned.1.call-start = ((), (), s32[]{:S(2)}) async-start(), calls=%async_computation.25 | async-start | bytes 3145728 | tf_op jit(solution)/shard_map/while/body/eval_jaxpr/reduce_scatter | solution.py:34
  2691.0 83.9 %reduce-scatter.12.cloned.1.call-start = ((), (), s32[]{:S(2)}) async-start(), calls=%async_computation.10 | async-start | bytes 294912 | tf_op jit(solution)/shard_map/reduce_scatter | solution.py:242
  2693.1 83.2 %reduce-scatter.10.cloned.1.call-start = ((), (), s32[]{:S(2)}) async-start(), calls=%async_computation.9 | async-start | bytes 884736 | tf_op jit(solution)/shard_map/reduce_scatter | solution.py:239
  2695.7 93.1 %reduce-scatter.14.cloned.1.call-start = ((), (), s32[]{:S(2)}) async-start(), calls=%async_computation.11 | async-start | bytes 1179648 | tf_op jit(solution)/shard_map/reduce_scatter | solution.py:245
  2698.7 123.0 %reduce-scatter.16.cloned.1.call-start = ((), (), s32[]{:S(2)}) async-start(), calls=%async_computation.12 | async-start | bytes 1179648 | tf_op jit(solution)/shard_map/reduce_scatter | solution.py:248
  (383 other events, 6389.8 us)
Sparse Core Ops, SparseCore 0:
  9.6 26.7 all-gather.14
  38.0 20.7 all-gather.12
  68.9 20.9 all-gather.16
  131.8 31.8 reduce-scatter.17
  169.1 21.2 all-gather.18
  204.1 31.8 reduce-scatter.19
  260.1 22.2 all-gather.16
  324.3 31.8 reduce-scatter.17
  361.6 21.2 all-gather.18
  396.6 31.8 reduce-scatter.19
  452.6 22.2 all-gather.16
  516.8 31.8 reduce-scatter.17
  554.1 21.2 all-gather.18
  589.1 31.8 reduce-scatter.19
  645.1 22.2 all-gather.16
  709.3 31.8 reduce-scatter.17
  746.6 21.2 all-gather.18
  781.6 31.8 reduce-scatter.19
  837.6 22.2 all-gather.16
  901.8 31.8 reduce-scatter.17
  939.1 21.2 all-gather.18
  974.1 31.8 reduce-scatter.19
  1057.2 22.2 all-gather.20
  1129.0 31.8 reduce-scatter.21
  1163.9 21.2 all-gather.22
  1186.7 21.2 all-gather.24
  1218.3 31.8 reduce-scatter.23
  1256.2 21.3 all-gather.26
  1326.9 31.8 reduce-scatter.25
  1386.8 20.3 all-gather.20
  1456.8 31.8 reduce-scatter.21
  1491.7 21.2 all-gather.22
  1514.5 21.2 all-gather.24
  1546.1 31.8 reduce-scatter.23
  1584.0 21.3 all-gather.26
  1654.7 31.8 reduce-scatter.25
  1714.6 20.3 all-gather.20
  1784.6 31.8 reduce-scatter.21
  1819.5 21.2 all-gather.22
  1842.5 21.2 all-gather.24
  1874.1 31.8 reduce-scatter.23
  1912.0 21.3 all-gather.26
  1982.7 31.8 reduce-scatter.25
  2042.6 20.3 all-gather.20
  2112.6 31.8 reduce-scatter.21
  2147.5 21.2 all-gather.22
  2170.3 21.2 all-gather.24
  2201.9 31.8 reduce-scatter.23
  2239.8 21.3 all-gather.26
  2310.5 31.8 reduce-scatter.25
  2370.4 20.3 all-gather.20
  2440.4 31.8 reduce-scatter.21
  2475.3 21.2 all-gather.22
  2498.2 21.2 all-gather.24
  2529.8 31.8 reduce-scatter.23
  2567.8 21.3 all-gather.26
  2638.4 31.8 reduce-scatter.25
  2694.3 29.5 reduce-scatter.11
  2726.1 29.6 reduce-scatter.9
  2758.1 30.6 reduce-scatter.13
  2791.1 30.5 reduce-scatter.15
where the time goes:
time: 2840 us; the launch traced here: 2830 us
  waiting for transfers between devices  1450 us (51%)
  matrix products  729 us (26%)
  other arithmetic  380 us (13%)
  blocking collectives  109 us (4%)
  local copies, waits for them, and re-layouts  83.2 us (3%)
  loops' own time  42.2 us (1%)
    reduce_scatter x15, waiting for transfers between devices, sum_columns(): lax.psum_scatter(partial_rows, 'col', scatter_dimension=0, tiled=True)  474 us
    all_gather x20, waiting for transfers between devices, spread_features(): return lax.all_gather(normed, 'col', axis=0, tiled=True)  388 us
    reduce_scatter x10, waiting for transfers between devices, sum_grad_columns(): lax.psum_scatter(partial_rows, 'col', scatter_dimension=0, tiled=True)  246 us
    sub x10, other arithmetic, attention_probs(): return jax.nn.softmax(scores, axis=-1)  158 us
    all_gather x10, waiting for transfers between devices, spread_grads(): return lax.all_gather(grad_low, 'col', axis=0, tiled=True)  158 us
    dot_general x10, matrix products, layer_forward(): jnp.einsum('hqk,khd->qhd', softmax_out.astype(jnp.bfloat16), value_heads,...  158 us
    ppermute x10, waiting for transfers between devices, from_behind(): lax.ppermute(value, axis, [(source, source + steps) for source in range(f...  126 us
    dot_general x5, matrix products, layer_backward(): jnp.einsum('qhd,khd->hqk', grad_context, value_heads, preferred_element_t...  82.3 us
  transfers between devices with their start and end apart: 71, of which 68 were waited for; matrix products, arithmetic and copies ran while one was open for 7% of the time, Pallas kernels for 0%

commit v1 on v0

--- a/solution.py
+++ b/solution.py
@@ -8,6 +8,18 @@
 epsilon = 1e-05
 
 
+def gather_by_bits(x, axis, dim):
+    ways, here = (lax.axis_size(axis), lax.axis_index(axis))
+    grown, reach = (x, 1)
+    while reach < ways:
+        theirs = lax.ppermute(grown, axis, [(d, d ^ reach) for d in range(ways)])
+        mine_first = jnp.concatenate([grown, theirs], axis=dim)
+        theirs_first = jnp.concatenate([theirs, grown], axis=dim)
+        grown = jnp.where(here & reach == 0, mine_first, theirs_first)
+        reach = 2 * reach
+    return grown
+
+
 def from_behind(value, axis, steps):
     count = lax.axis_size(axis)
     first, last = (max(0, -steps), min(count, count - steps))
@@ -19,7 +31,7 @@
 
 
 def spread_features(normed):
-    return lax.all_gather(normed, "col", axis=0, tiled=True)
+    return gather_by_bits(normed, "col", 0)
 
 
 def sum_columns(partial_rows):

time: 2840 us -> 2620 us (0.923)
  waiting for transfers between devices: 1450 us -> 1200 us
    all_gather x20 -> x0, waiting for transfers between devices: 388 us -> none  [spread_features(): return lax.all_gather(normed, 'col', axis=0, tiled=True)]
    ppermute x0 -> x20, waiting for transfers between devices: none -> 203 us  [gather_by_bits(): theirs = lax.ppermute(grown, axis, [(d, d ^ reach) for d in range(ways)])]
    all_gather x10, waiting for transfers between devices: 158 us -> 107 us  [spread_grads(): return lax.all_gather(grad_low, 'col', axis=0, tiled=True)]
  transfers between devices with their start and end apart: 71 -> 71, of which waited for: 68 -> 63; matrix products, arithmetic and copies ran while one was open for 7% -> 8% of each run, Pallas kernels for 0% -> 0%
where the time goes in v1:
time: 2620 us
  waiting for transfers between devices  1200 us (46%)
  matrix products  738 us (28%)
  other arithmetic  383 us (15%)
  blocking collectives  109 us (4%)
  local copies, waits for them, and re-layouts  89.5 us (3%)
  loops' own time  41.5 us (2%)
  starting transfers between devices  35.5 us (1%)
    reduce_scatter x15, waiting for transfers between devices, sum_columns(): lax.psum_scatter(partial_rows, 'col', scatter_dimension=0, tiled=True)  475 us
    reduce_scatter x10, waiting for transfers between devices, sum_grad_columns(): lax.psum_scatter(partial_rows, 'col', scatter_dimension=0, tiled=True)  243 us
    ppermute x20, waiting for transfers between devices, gather_by_bits(): theirs = lax.ppermute(grown, axis, [(d, d ^ reach) for d in range(ways)])  203 us
    sub x10, other arithmetic, attention_probs(): return jax.nn.softmax(scores, axis=-1)  158 us
    dot_general x10, matrix products, layer_forward(): jnp.einsum('hqk,khd->qhd', softmax_out.astype(jnp.bfloat16), value_heads,...  156 us
    ppermute x10, waiting for transfers between devices, from_behind(): lax.ppermute(value, axis, [(source, source + steps) for source in range(f...  124 us
    all_gather x10, waiting for transfers between devices, spread_grads(): return lax.all_gather(grad_low, 'col', axis=0, tiled=True)  107 us
    dot_general x5, matrix products, layer_backward(): jnp.einsum('qhd,khd->hqk', grad_context, value_heads, preferred_element_t...  82.3 us
  transfers between devices with their start and end apart: 71, of which 63 were waited for; matrix products, arithmetic and copies ran while one was open for 8% of the time, Pallas kernels for 0%

profile of v1, /device:TPU:0, one launch (start us, length us, event | category | flops | bytes accessed | tf_op | source)
XLA Modules:
  0.0 2616.2 jit_solution(7384518971983356016)
XLA Ops:
  8.8 16.2 all-gather.1
  25.8 18.5 all-gather
  61.8 875.9 %while.55 = (s32[]{:T(128)}, bf16[512,512]{1,0:T(8,128)(2,1)S(1)}, bf16[4,512,512]{2,1,0:T(8,128)(2,1)}, bf16[4,512,512]{2,1,0:T(8,128)(2,1)}, pred[]{:T(512)}, ...) while((s32[]{:T(128)}, bf16[512,512]{1,0:T(8,128)(2,1)S(1)}, ...), condition=%wide.region_9.10_spmd, body=%wide.region_0.9_spmd.sunk | while | flops 4422900736 | bytes 123835592 | solution.py:327
  105.9 15.6 fusion.273
  124.3 31.6 %reduce-scatter.18.cloned.1.call-done = f32[512,512]{1,0:T(8,128)} async-done(((f32[1024,512]{1,0:T(8,128)}), f32[512,512]{1,0:T(8,128)}) %reduce-scatter.18.cloned.1.call-update) | async-done | bytes 1048592 | tf_op jit(solution)/shard_map/while/body/eval_jaxpr/reduce_scatter | solution.py:38
  189.3 30.9 %reduce-scatter.20.cloned.1.call-done = f32[512,512]{1,0:T(8,128)} async-done(((f32[1024,512]{1,0:T(8,128)}), f32[512,512]{1,0:T(8,128)}) %reduce-scatter.20.cloned.1.call-update) | async-done | bytes 1048592 | tf_op jit(solution)/shard_map/while/body/eval_jaxpr/reduce_scatter | solution.py:38
  279.7 15.6 fusion.273
  298.1 32.9 %reduce-scatter.18.cloned.1.call-done = f32[512,512]{1,0:T(8,128)} async-done(((f32[1024,512]{1,0:T(8,128)}), f32[512,512]{1,0:T(8,128)}) %reduce-scatter.18.cloned.1.call-update) | async-done | bytes 1048592 | tf_op jit(solution)/shard_map/while/body/eval_jaxpr/reduce_scatter | solution.py:38
  364.5 30.9 %reduce-scatter.20.cloned.1.call-done = f32[512,512]{1,0:T(8,128)} async-done(((f32[1024,512]{1,0:T(8,128)}), f32[512,512]{1,0:T(8,128)}) %reduce-scatter.20.cloned.1.call-update) | async-done | bytes 1048592 | tf_op jit(solution)/shard_map/while/body/eval_jaxpr/reduce_scatter | solution.py:38
  454.8 15.6 fusion.273
  473.2 32.9 %reduce-scatter.18.cloned.1.call-done = f32[512,512]{1,0:T(8,128)} async-done(((f32[1024,512]{1,0:T(8,128)}), f32[512,512]{1,0:T(8,128)}) %reduce-scatter.18.cloned.1.call-update) | async-done | bytes 1048592 | tf_op jit(solution)/shard_map/while/body/eval_jaxpr/reduce_scatter | solution.py:38
  539.6 30.9 %reduce-scatter.20.cloned.1.call-done = f32[512,512]{1,0:T(8,128)} async-done(((f32[1024,512]{1,0:T(8,128)}), f32[512,512]{1,0:T(8,128)}) %reduce-scatter.20.cloned.1.call-update) | async-done | bytes 1048592 | tf_op jit(solution)/shard_map/while/body/eval_jaxpr/reduce_scatter | solution.py:38
  629.9 15.6 fusion.273
  648.4 33.0 %reduce-scatter.18.cloned.1.call-done = f32[512,512]{1,0:T(8,128)} async-done(((f32[1024,512]{1,0:T(8,128)}), f32[512,512]{1,0:T(8,128)}) %reduce-scatter.18.cloned.1.call-update) | async-done | bytes 1048592 | tf_op jit(solution)/shard_map/while/body/eval_jaxpr/reduce_scatter | solution.py:38
  714.8 30.9 %reduce-scatter.20.cloned.1.call-done = f32[512,512]{1,0:T(8,128)} async-done(((f32[1024,512]{1,0:T(8,128)}), f32[512,512]{1,0:T(8,128)}) %reduce-scatter.20.cloned.1.call-update) | async-done | bytes 1048592 | tf_op jit(solution)/shard_map/while/body/eval_jaxpr/reduce_scatter | solution.py:38
  805.1 15.6 fusion.273
  823.5 33.0 %reduce-scatter.18.cloned.1.call-done = f32[512,512]{1,0:T(8,128)} async-done(((f32[1024,512]{1,0:T(8,128)}), f32[512,512]{1,0:T(8,128)}) %reduce-scatter.18.cloned.1.call-update) | async-done | bytes 1048592 | tf_op jit(solution)/shard_map/while/body/eval_jaxpr/reduce_scatter | solution.py:38
  889.9 30.9 %reduce-scatter.20.cloned.1.call-done = f32[512,512]{1,0:T(8,128)} async-done(((f32[1024,512]{1,0:T(8,128)}), f32[512,512]{1,0:T(8,128)}) %reduce-scatter.20.cloned.1.call-update) | async-done | bytes 1048592 | tf_op jit(solution)/shard_map/while/body/eval_jaxpr/reduce_scatter | solution.py:38
  940.9 1535.9 %while.56 = (s32[]{:T(128)}, bf16[512,512]{1,0:T(8,128)(2,1)S(1)}, f32[4,512,512]{2,1,0:T(8,128)}, f32[3,512,256]{1,2,0:T(8,128)}, f32[256,512]{1,0:T(8,128)}, /...) while((s32[]{:T(128)}, bf16[512,512]{1,0:T(8,128)(2,1)S(1)}, ...), condition=%wide.region_34.35_spmd.clone, body=%wide.region_10.34_spmd.clone.sunk | while | flops 12035830784 | bytes 494568288 | solution.py:360
  994.2 19.1 fusion.307
  1013.3 15.6 fusion.308
  1032.0 32.9 %reduce-scatter.22.cloned.1.call-done = f32[512,512]{1,0:T(8,128)} async-done(((f32[1024,512]{1,0:T(8,128)}), f32[512,512]{1,0:T(8,128)}) %reduce-scatter.22.cloned.1.call-update) | async-done | bytes 1048592 | tf_op jit(solution)/shard_map/while/body/eval_jaxpr/reduce_scatter | solution.py:38
  1106.1 32.0 %reduce-scatter.24.cloned.1.call-done = f32[512,512]{1,0:T(8,128)} async-done(((f32[1024,512]{1,0:T(8,128)}), f32[512,512]{1,0:T(8,128)}) %reduce-scatter.24.cloned.1.call-update) | async-done | bytes 1048592 | tf_op jit(solution)/shard_map/while/body/eval_jaxpr/reduce_scatter | solution.py:46
  1143.9 21.4 all-gather.15.cloned.1.call-done
  1167.0 14.3 fusion.316
  1181.4 16.5 multiply_reduce_fusion.16
  1229.2 18.2 reduce-scatter.26.cloned.1.call-done
  1298.4 19.1 fusion.307
  1317.5 15.6 fusion.308
  1336.1 31.0 %reduce-scatter.22.cloned.1.call-done = f32[512,512]{1,0:T(8,128)} async-done(((f32[1024,512]{1,0:T(8,128)}), f32[512,512]{1,0:T(8,128)}) %reduce-scatter.22.cloned.1.call-update) | async-done | bytes 1048592 | tf_op jit(solution)/shard_map/while/body/eval_jaxpr/reduce_scatter | solution.py:38
  1408.3 32.0 %reduce-scatter.24.cloned.1.call-done = f32[512,512]{1,0:T(8,128)} async-done(((f32[1024,512]{1,0:T(8,128)}), f32[512,512]{1,0:T(8,128)}) %reduce-scatter.24.cloned.1.call-update) | async-done | bytes 1048592 | tf_op jit(solution)/shard_map/while/body/eval_jaxpr/reduce_scatter | solution.py:46
  1446.1 21.4 all-gather.15.cloned.1.call-done
  1469.3 14.3 fusion.316
  1483.6 16.5 multiply_reduce_fusion.16
  1533.5 16.1 reduce-scatter.26.cloned.1.call-done
  1556.5 13.6 collective-permute-done.5
  1600.6 19.1 fusion.307
  1619.7 15.6 fusion.308
  1638.3 31.0 %reduce-scatter.22.cloned.1.call-done = f32[512,512]{1,0:T(8,128)} async-done(((f32[1024,512]{1,0:T(8,128)}), f32[512,512]{1,0:T(8,128)}) %reduce-scatter.22.cloned.1.call-update) | async-done | bytes 1048592 | tf_op jit(solution)/shard_map/while/body/eval_jaxpr/reduce_scatter | solution.py:38
  1710.5 32.0 %reduce-scatter.24.cloned.1.call-done = f32[512,512]{1,0:T(8,128)} async-done(((f32[1024,512]{1,0:T(8,128)}), f32[512,512]{1,0:T(8,128)}) %reduce-scatter.24.cloned.1.call-update) | async-done | bytes 1048592 | tf_op jit(solution)/shard_map/while/body/eval_jaxpr/reduce_scatter | solution.py:46
  1748.3 21.4 all-gather.15.cloned.1.call-done
  1771.5 14.3 fusion.316
  1785.8 16.5 multiply_reduce_fusion.16
  1835.7 16.1 reduce-scatter.26.cloned.1.call-done
  1902.8 19.1 fusion.307
  1921.9 15.6 fusion.308
  1940.5 31.0 %reduce-scatter.22.cloned.1.call-done = f32[512,512]{1,0:T(8,128)} async-done(((f32[1024,512]{1,0:T(8,128)}), f32[512,512]{1,0:T(8,128)}) %reduce-scatter.22.cloned.1.call-update) | async-done | bytes 1048592 | tf_op jit(solution)/shard_map/while/body/eval_jaxpr/reduce_scatter | solution.py:38
  2012.7 32.0 %reduce-scatter.24.cloned.1.call-done = f32[512,512]{1,0:T(8,128)} async-done(((f32[1024,512]{1,0:T(8,128)}), f32[512,512]{1,0:T(8,128)}) %reduce-scatter.24.cloned.1.call-update) | async-done | bytes 1048592 | tf_op jit(solution)/shard_map/while/body/eval_jaxpr/reduce_scatter | solution.py:46
  2050.5 21.4 all-gather.15.cloned.1.call-done
  2073.7 14.3 fusion.316
  2088.0 16.5 multiply_reduce_fusion.16
  2138.0 16.1 reduce-scatter.26.cloned.1.call-done
  2160.9 13.6 collective-permute-done.5
  2205.0 19.1 fusion.307
  2224.2 15.6 fusion.308
  2242.8 31.0 %reduce-scatter.22.cloned.1.call-done = f32[512,512]{1,0:T(8,128)} async-done(((f32[1024,512]{1,0:T(8,128)}), f32[512,512]{1,0:T(8,128)}) %reduce-scatter.22.cloned.1.call-update) | async-done | bytes 1048592 | tf_op jit(solution)/shard_map/while/body/eval_jaxpr/reduce_scatter | solution.py:38
  2314.9 32.0 %reduce-scatter.24.cloned.1.call-done = f32[512,512]{1,0:T(8,128)} async-done(((f32[1024,512]{1,0:T(8,128)}), f32[512,512]{1,0:T(8,128)}) %reduce-scatter.24.cloned.1.call-update) | async-done | bytes 1048592 | tf_op jit(solution)/shard_map/while/body/eval_jaxpr/reduce_scatter | solution.py:46
  2352.8 21.4 all-gather.15.cloned.1.call-done
  2375.9 14.3 fusion.316
  2390.3 16.5 multiply_reduce_fusion.16
  2440.2 16.1 reduce-scatter.26.cloned.1.call-done
  2486.1 16.3 all-reduce.1
  2502.4 58.3 %all-reduce = (f32[1,512]{1,0:T(1,128)}, f32[1,512]{1,0:T(1,128)}, f32[1,512]{1,0:T(1,128)}, f32[1,512]{1,0:T(1,128)}, f32[1,512]{1,0:T(1,128)}, /*index=5*/f32[1,512]{1,0:T(1,128)}) all-reduce(f32[1,512]{1,0:T(1,128)S(1)} %bitcast.353, f32[1,512]{1,0:T(1,128)S(1)} %bitcast.352, ...), channel_id=1, replica_groups=mesh['pipe'=2,'row'=8,'col'=2] {'row','col'}, use_global_device_ids=true, to_apply=%region_35.36 | all-reduce | flops 3072 | bytes 24576 | tf_op jit(solution)/shard_map/psum | solution.py:366
  2576.6 30.7 %reduce-scatter.16.cloned.1.call-done = bf16[1024,64]{0,1:T(8,128)(2,1)} async-done(((bf16[1024,512]{0,1:T(8,128)(2,1)}), bf16[1024,64]{0,1:T(8,128)(2,1)}) %reduce-scatter.16.cloned.1.call-update) | async-done | bytes 131088 | tf_op jit(solution)/shard_map/reduce_scatter | solution.py:260
  (1283 shorter events, 1162.7 us)
Async XLA Ops:
  7.2 39.5 %all-gather.11.cloned.1.call-start = ((), (), s32[]{:S(2)}) async-start(), calls=%async_computation.14 | async-start | bytes 1179648 | tf_op jit(solution)/shard_map/all_gather | solution.py:292
  7.9 50.9 %all-gather.9.cloned.1.call-start = ((), (), s32[]{:S(2)}) async-start(), calls=%async_computation.13 | async-start | bytes 1179648 | tf_op jit(solution)/shard_map/all_gather | solution.py:291
  62.0 93.8 %reduce-scatter.18.cloned.1.call-start = ((), (), s32[]{:S(2)}) async-start(), calls=%async_computation.15 | async-start | bytes 3145728 | tf_op jit(solution)/shard_map/while/body/eval_jaxpr/reduce_scatter | solution.py:38
  68.6 14.1 collective-permute-start
  124.2 96.0 %reduce-scatter.20.cloned.1.call-start = ((), (), s32[]{:S(2)}) async-start(), calls=%async_computation.16 | async-start | bytes 3145728 | tf_op jit(solution)/shard_map/while/body/eval_jaxpr/reduce_scatter | solution.py:38
  160.4 13.7 collective-permute-start.1
  222.6 14.5 collective-permute-start.2
  237.1 93.9 %reduce-scatter.18.cloned.1.call-start = ((), (), s32[]{:S(2)}) async-start(), calls=%async_computation.15 | async-start | bytes 3145728 | tf_op jit(solution)/shard_map/while/body/eval_jaxpr/reduce_scatter | solution.py:38
  298.0 97.3 %reduce-scatter.20.cloned.1.call-start = ((), (), s32[]{:S(2)}) async-start(), calls=%async_computation.16 | async-start | bytes 3145728 | tf_op jit(solution)/shard_map/while/body/eval_jaxpr/reduce_scatter | solution.py:38
  335.5 13.7 collective-permute-start.1
  397.8 14.5 collective-permute-start.2
  412.3 93.9 %reduce-scatter.18.cloned.1.call-start = ((), (), s32[]{:S(2)}) async-start(), calls=%async_computation.15 | async-start | bytes 3145728 | tf_op jit(solution)/shard_map/while/body/eval_jaxpr/reduce_scatter | solution.py:38
  418.8 12.9 collective-permute-start
  473.2 97.3 %reduce-scatter.20.cloned.1.call-start = ((), (), s32[]{:S(2)}) async-start(), calls=%async_computation.16 | async-start | bytes 3145728 | tf_op jit(solution)/shard_map/while/body/eval_jaxpr/reduce_scatter | solution.py:38
  510.7 13.7 collective-permute-start.1
  572.9 14.5 collective-permute-start.2
  587.4 93.9 %reduce-scatter.18.cloned.1.call-start = ((), (), s32[]{:S(2)}) async-start(), calls=%async_computation.15 | async-start | bytes 3145728 | tf_op jit(solution)/shard_map/while/body/eval_jaxpr/reduce_scatter | solution.py:38
  648.3 97.4 %reduce-scatter.20.cloned.1.call-start = ((), (), s32[]{:S(2)}) async-start(), calls=%async_computation.16 | async-start | bytes 3145728 | tf_op jit(solution)/shard_map/while/body/eval_jaxpr/reduce_scatter | solution.py:38
  685.8 13.8 collective-permute-start.1
  748.0 14.5 collective-permute-start.2
  762.6 93.9 %reduce-scatter.18.cloned.1.call-start = ((), (), s32[]{:S(2)}) async-start(), calls=%async_computation.15 | async-start | bytes 3145728 | tf_op jit(solution)/shard_map/while/body/eval_jaxpr/reduce_scatter | solution.py:38
  823.4 97.4 %reduce-scatter.20.cloned.1.call-start = ((), (), s32[]{:S(2)}) async-start(), calls=%async_computation.16 | async-start | bytes 3145728 | tf_op jit(solution)/shard_map/while/body/eval_jaxpr/reduce_scatter | solution.py:38
  861.0 13.7 collective-permute-start.1
  923.2 14.5 collective-permute-start.2
  963.8 101.2 %reduce-scatter.22.cloned.1.call-start = ((), (), s32[]{:S(2)}) async-start(), calls=%async_computation.17 | async-start | bytes 3145728 | tf_op jit(solution)/shard_map/while/body/eval_jaxpr/reduce_scatter | solution.py:38
  969.6 12.9 collective-permute-start.3
  1031.9 63.9 %all-gather.13.cloned.1.call-start = ((), (), s32[]{:S(2)}) async-start(), calls=%async_computation.18 | async-start | bytes 1572864 | tf_op jit(solution)/shard_map/while/body/eval_jaxpr/all_gather | solution.py:42
  1067.7 13.7 collective-permute-start.4
  1072.1 66.0 %reduce-scatter.24.cloned.1.call-start = ((), (), s32[]{:S(2)}) async-start(), calls=%async_computation.19 | async-start | bytes 3145728 | tf_op jit(solution)/shard_map/while/body/eval_jaxpr/reduce_scatter | solution.py:46
  1106.0 59.3 %all-gather.15.cloned.1.call-start = ((), (), s32[]{:S(2)}) async-start(), calls=%async_computation.20 | async-start | bytes 1572864 | tf_op jit(solution)/shard_map/while/body/eval_jaxpr/all_gather | solution.py:42
  1143.8 103.6 %reduce-scatter.26.cloned.1.call-start = ((), (), s32[]{:S(2)}) async-start(), calls=%async_computation.21 | async-start | bytes 3145728 | tf_op jit(solution)/shard_map/while/body/eval_jaxpr/reduce_scatter | solution.py:46
  1252.3 15.5 collective-permute-start.5
  1267.9 99.2 %reduce-scatter.22.cloned.1.call-start = ((), (), s32[]{:S(2)}) async-start(), calls=%async_computation.17 | async-start | bytes 3145728 | tf_op jit(solution)/shard_map/while/body/eval_jaxpr/reduce_scatter | solution.py:38
  1336.1 62.0 %all-gather.13.cloned.1.call-start = ((), (), s32[]{:S(2)}) async-start(), calls=%async_computation.18 | async-start | bytes 1572864 | tf_op jit(solution)/shard_map/while/body/eval_jaxpr/all_gather | solution.py:42
  1370.0 13.7 collective-permute-start.4
  1374.3 65.9 %reduce-scatter.24.cloned.1.call-start = ((), (), s32[]{:S(2)}) async-start(), calls=%async_computation.19 | async-start | bytes 3145728 | tf_op jit(solution)/shard_map/while/body/eval_jaxpr/reduce_scatter | solution.py:46
  1408.2 59.3 %all-gather.15.cloned.1.call-start = ((), (), s32[]{:S(2)}) async-start(), calls=%async_computation.20 | async-start | bytes 1572864 | tf_op jit(solution)/shard_map/while/body/eval_jaxpr/all_gather | solution.py:42
  1446.0 103.6 %reduce-scatter.26.cloned.1.call-start = ((), (), s32[]{:S(2)}) async-start(), calls=%async_computation.21 | async-start | bytes 3145728 | tf_op jit(solution)/shard_map/while/body/eval_jaxpr/reduce_scatter | solution.py:46
  1554.5 15.5 collective-permute-start.5
  1570.1 99.2 %reduce-scatter.22.cloned.1.call-start = ((), (), s32[]{:S(2)}) async-start(), calls=%async_computation.17 | async-start | bytes 3145728 | tf_op jit(solution)/shard_map/while/body/eval_jaxpr/reduce_scatter | solution.py:38
  1638.3 62.0 %all-gather.13.cloned.1.call-start = ((), (), s32[]{:S(2)}) async-start(), calls=%async_computation.18 | async-start | bytes 1572864 | tf_op jit(solution)/shard_map/while/body/eval_jaxpr/all_gather | solution.py:42
  1672.2 13.7 collective-permute-start.4
  1676.5 66.0 %reduce-scatter.24.cloned.1.call-start = ((), (), s32[]{:S(2)}) async-start(), calls=%async_computation.19 | async-start | bytes 3145728 | tf_op jit(solution)/shard_map/while/body/eval_jaxpr/reduce_scatter | solution.py:46
  1710.4 59.3 %all-gather.15.cloned.1.call-start = ((), (), s32[]{:S(2)}) async-start(), calls=%async_computation.20 | async-start | bytes 1572864 | tf_op jit(solution)/shard_map/while/body/eval_jaxpr/all_gather | solution.py:42
  1748.3 103.6 %reduce-scatter.26.cloned.1.call-start = ((), (), s32[]{:S(2)}) async-start(), calls=%async_computation.21 | async-start | bytes 3145728 | tf_op jit(solution)/shard_map/while/body/eval_jaxpr/reduce_scatter | solution.py:46
  1856.8 15.5 collective-permute-start.5
  1872.3 99.2 %reduce-scatter.22.cloned.1.call-start = ((), (), s32[]{:S(2)}) async-start(), calls=%async_computation.17 | async-start | bytes 3145728 | tf_op jit(solution)/shard_map/while/body/eval_jaxpr/reduce_scatter | solution.py:38
  1940.5 62.0 %all-gather.13.cloned.1.call-start = ((), (), s32[]{:S(2)}) async-start(), calls=%async_computation.18 | async-start | bytes 1572864 | tf_op jit(solution)/shard_map/while/body/eval_jaxpr/all_gather | solution.py:42
  1974.4 13.7 collective-permute-start.4
  1978.7 66.0 %reduce-scatter.24.cloned.1.call-start = ((), (), s32[]{:S(2)}) async-start(), calls=%async_computation.19 | async-start | bytes 3145728 | tf_op jit(solution)/shard_map/while/body/eval_jaxpr/reduce_scatter | solution.py:46
  2012.7 59.3 %all-gather.15.cloned.1.call-start = ((), (), s32[]{:S(2)}) async-start(), calls=%async_computation.20 | async-start | bytes 1572864 | tf_op jit(solution)/shard_map/while/body/eval_jaxpr/all_gather | solution.py:42
  2050.5 103.6 %reduce-scatter.26.cloned.1.call-start = ((), (), s32[]{:S(2)}) async-start(), calls=%async_computation.21 | async-start | bytes 3145728 | tf_op jit(solution)/shard_map/while/body/eval_jaxpr/reduce_scatter | solution.py:46
  2159.0 15.5 collective-permute-start.5
  2174.6 99.2 %reduce-scatter.22.cloned.1.call-start = ((), (), s32[]{:S(2)}) async-start(), calls=%async_computation.17 | async-start | bytes 3145728 | tf_op jit(solution)/shard_map/while/body/eval_jaxpr/reduce_scatter | solution.py:38
  2242.7 62.0 %all-gather.13.cloned.1.call-start = ((), (), s32[]{:S(2)}) async-start(), calls=%async_computation.18 | async-start | bytes 1572864 | tf_op jit(solution)/shard_map/while/body/eval_jaxpr/all_gather | solution.py:42
  2276.6 13.7 collective-permute-start.4
  2281.0 66.0 %reduce-scatter.24.cloned.1.call-start = ((), (), s32[]{:S(2)}) async-start(), calls=%async_computation.19 | async-start | bytes 3145728 | tf_op jit(solution)/shard_map/while/body/eval_jaxpr/reduce_scatter | solution.py:46
  2314.9 59.3 %all-gather.15.cloned.1.call-start = ((), (), s32[]{:S(2)}) async-start(), calls=%async_computation.20 | async-start | bytes 1572864 | tf_op jit(solution)/shard_map/while/body/eval_jaxpr/all_gather | solution.py:42
  2352.7 103.6 %reduce-scatter.26.cloned.1.call-start = ((), (), s32[]{:S(2)}) async-start(), calls=%async_computation.21 | async-start | bytes 3145728 | tf_op jit(solution)/shard_map/while/body/eval_jaxpr/reduce_scatter | solution.py:46
  2461.2 15.5 collective-permute-start.5
  2476.8 84.0 %reduce-scatter.12.cloned.1.call-start = ((), (), s32[]{:S(2)}) async-start(), calls=%async_computation.10 | async-start | bytes 294912 | tf_op jit(solution)/shard_map/reduce_scatter | solution.py:254
  2478.9 83.2 %reduce-scatter.10.cloned.1.call-start = ((), (), s32[]{:S(2)}) async-start(), calls=%async_computation.9 | async-start | bytes 884736 | tf_op jit(solution)/shard_map/reduce_scatter | solution.py:251
  2481.6 93.4 %reduce-scatter.14.cloned.1.call-start = ((), (), s32[]{:S(2)}) async-start(), calls=%async_computation.11 | async-start | bytes 1179648 | tf_op jit(solution)/shard_map/reduce_scatter | solution.py:257
  2484.5 122.8 %reduce-scatter.16.cloned.1.call-start = ((), (), s32[]{:S(2)}) async-start(), calls=%async_computation.12 | async-start | bytes 1179648 | tf_op jit(solution)/shard_map/reduce_scatter | solution.py:260
  (353 other events, 4147.9 us)
Sparse Core Ops, SparseCore 0:
  9.6 26.7 all-gather.10
  38.0 20.7 all-gather.8
  124.4 31.4 reduce-scatter.17
  188.4 31.8 reduce-scatter.19
  298.2 32.8 reduce-scatter.17
  363.5 31.8 reduce-scatter.19
  473.3 32.8 reduce-scatter.17
  538.6 31.8 reduce-scatter.19
  648.4 32.8 reduce-scatter.17
  713.8 31.8 reduce-scatter.19
  823.6 32.8 reduce-scatter.17
  889.0 31.8 reduce-scatter.19
  1032.0 32.8 reduce-scatter.21
  1072.2 22.4 all-gather.12
  1106.1 31.8 reduce-scatter.23
  1143.9 21.2 all-gather.14
  1215.6 31.8 reduce-scatter.25
  1336.2 30.9 reduce-scatter.21
  1374.4 22.4 all-gather.12
  1408.4 31.8 reduce-scatter.23
  1446.1 21.2 all-gather.14
  1517.8 31.8 reduce-scatter.25
  1638.4 30.9 reduce-scatter.21
  1676.7 22.4 all-gather.12
  1710.6 31.8 reduce-scatter.23
  1748.4 21.2 all-gather.14
  1820.0 31.8 reduce-scatter.25
  1940.6 30.9 reduce-scatter.21
  1978.9 22.4 all-gather.12
  2012.8 31.8 reduce-scatter.23
  2050.6 21.2 all-gather.14
  2122.2 31.8 reduce-scatter.25
  2242.8 30.9 reduce-scatter.21
  2281.1 22.4 all-gather.12
  2315.0 31.8 reduce-scatter.23
  2352.8 21.2 all-gather.14
  2424.5 31.8 reduce-scatter.25
  2480.4 29.4 reduce-scatter.11
  2512.2 29.7 reduce-scatter.9
  2544.3 30.6 reduce-scatter.13
  2577.2 30.0 reduce-scatter.15
